TPU v7x, 128 devices: a whole 4x4x4 slice. The times are simulated.
128 devices in a mesh: group: 16 (over x_hi, y, core), mp: 8 (over z, x_lo).
Axes of the slice: x: 4 (x_hi: 2, x_lo: 2; x = x_hi * 2 + x_lo), y: 4, z: 4, core: 2. Of those that a mesh axis runs over, the one named last changes fastest.
Arguments:
- tokens: bfloat16 [2, 2048, 8192], P(None, 'group'), may hold values from -6 to 6
- q_weight: bfloat16 [8192, 8192], P('group', 'mp'), may hold values from -0.0625 to 0.0625
- kv_weight: bfloat16 [8192, 2048], P('group', 'mp'), may hold values from -0.0625 to 0.0625
- o_weight: bfloat16 [8192, 8192], P('mp', 'group'), may hold values from -0.5 to 0.5
- kv_pool: bfloat16 [16384, 16, 2048], P('group', None, 'mp'), may hold values from -51 to 51
- send_list: int32 [16, 16, 8], P('group'), may hold values from 0 to 1023
- page_table: int32 [2048, 8], P('group'), may hold values from 0 to 1151
- lengths: int32 [2048], P('group'), may hold values from 1 to 128
Outputs:
- mixed: bfloat16 [2, 2048, 8192], P(None, 'group', 'mp')
Inputs may be any that keep to these rules, and one draw needn't show every extreme that they name: `page_table`: entries below 1024 name a page of the group index's own pool; entry 1024 + s * 8 + c names the page that source s sends in slot c. `send_list`: page ids of the sending group index's own pool; a page may be named more than once.
All inputs are finite; a program needn't handle non-finite values.
Results may differ from a plain program's by a relative error of at most 0.018.
Values may be sent and summed in bfloat16 or wider, within the bound.
A program may use at most 192 MiB of HBM per device.

v0:
```python
import jax
import jax.numpy as jnp
from jax import lax
from jax.sharding import PartitionSpec as P

HD = 128


def stored(value):
    return lax.optimization_barrier(value.astype(jnp.bfloat16)).astype(jnp.float32)


def rotate(values, position):
    half = values.shape[-1] // 2
    inverse = 500000.0 ** (-(jnp.arange(half, dtype=jnp.float32) * 2.0) / (2.0 * half))
    angle = position[..., None] * inverse
    cosine = jnp.cos(angle)
    sine = jnp.sin(angle)
    first = values[..., :half]
    second = values[..., half:]
    return jnp.concatenate(
        [first * cosine - second * sine, second * cosine + first * sine], axis=-1
    )


def per_device(tokens, q_weight, kv_weight, o_weight, kv_pool, send_list, page_table, lengths):
    rows = tokens.shape[1]
    flat = tokens.reshape(2 * rows, tokens.shape[2])
    heads_here = q_weight.shape[1] // HD
    kv_here = kv_weight.shape[1] // (2 * HD)

    def add_rows(piece):
        return jnp.dot(flat, piece, preferred_element_type=jnp.float32)

    query = add_rows(lax.all_gather(q_weight, "group", axis=0, tiled=True))
    keyval = add_rows(lax.all_gather(kv_weight, "group", axis=0, tiled=True))
    position = lengths[None, :].astype(jnp.float32) + jnp.arange(2, dtype=jnp.float32)[:, None]
    query = rotate(query.reshape(2, rows, heads_here, HD), position[:, :, None]).astype(
        jnp.bfloat16
    )
    keyval = keyval.reshape(2, rows, kv_here, 2, HD)
    key_new = rotate(keyval[:, :, :, 0], position[:, :, None]).astype(jnp.bfloat16)
    value_new = keyval[:, :, :, 1].astype(jnp.bfloat16)
    outgoing = kv_pool[send_list[0]]
    arrived = lax.all_to_all(outgoing, "group", split_axis=0, concat_axis=0, tiled=True)
    held = jnp.concatenate([kv_pool, arrived.reshape((-1,) + kv_pool.shape[1:])], axis=0)
    context = page_table.shape[1] * kv_pool.shape[1]
    cache = held[page_table].reshape(rows, context, kv_here, 2, HD)
    key_cache = cache[:, :, :, 0]
    value_cache = cache[:, :, :, 1]
    grouped = query.reshape(2, rows, kv_here, heads_here // kv_here, HD)
    scale = 1.0 / HD**0.5
    score_cache = (
        jnp.einsum("trkgd,rckd->trkgc", grouped, key_cache, preferred_element_type=jnp.float32)
        * scale
    )
    live = jnp.arange(context)[None, :] < lengths[:, None]
    score_cache = jnp.where(live[None, :, None, None, :], score_cache, -jnp.inf)
    score_new = (
        jnp.einsum("trkgd,urkd->trkgu", grouped, key_new, preferred_element_type=jnp.float32)
        * scale
    )
    causal = jnp.arange(2)[:, None] >= jnp.arange(2)[None, :]
    score_new = jnp.where(causal[:, None, None, None, :], score_new, -jnp.inf)
    top = jnp.maximum(jnp.max(score_cache, axis=-1), jnp.max(score_new, axis=-1))
    exp_cache = jnp.exp(score_cache - top[..., None])
    exp_new = jnp.exp(score_new - top[..., None])
    total = jnp.sum(exp_cache, axis=-1) + jnp.sum(exp_new, axis=-1)
    numer = jnp.einsum(
        "trkgc,rckd->trkgd",
        exp_cache.astype(jnp.bfloat16),
        value_cache,
        preferred_element_type=jnp.float32,
    )
    numer = numer + jnp.einsum(
        "trkgu,urkd->trkgd",
        exp_new.astype(jnp.bfloat16),
        value_new,
        preferred_element_type=jnp.float32,
    )
    attn = (numer / total[..., None]).reshape(2 * rows, heads_here * HD).astype(jnp.bfloat16)
    partial_term = stored(
        jnp.dot(
            attn,
            lax.all_gather(o_weight, "group", axis=1, tiled=True),
            preferred_element_type=jnp.float32,
        )
    )
    mixed = lax.psum_scatter(
        partial_term.astype(jnp.bfloat16), "mp", scatter_dimension=1, tiled=True
    )
    return mixed.reshape(2, rows, -1)


def solution(mesh):
    in_specs = (
        P(None, "group", None),
        P("group", "mp"),
        P("group", "mp"),
        P("mp", "group"),
        P("group", None, "mp"),
        P("group", None, None),
        P("group", None),
        P("group"),
    )
    out_specs = P(None, "group", "mp")
    return jax.shard_map(
        per_device, mesh=mesh, in_specs=in_specs, out_specs=out_specs, check_vma=False
    )
```

profile of v0, /device:TPU:30, one launch (start us, length us, event | category | flops | bytes accessed | tf_op | source)
XLA Modules:
  0.0 409.9 jit_solution(17526062529710377650)
XLA Ops:
  6.5 0.0 all-gather.6.cloned.1.call-start
  6.5 0.7 all-gather.6.cloned.1.call-update
  7.3 0.0 all-gather.4.cloned.1.call-start
  7.3 0.7 all-gather.4.cloned.1.call-update
  8.0 0.0 all-gather.8.cloned.1.call-start
  8.1 0.7 all-gather.8.cloned.1.call-update
  8.7 0.7 compare_select_fusion.1
  9.4 0.1 copy.16
  9.5 0.1 reshape.224
  9.6 5.0 %gather_fusion = bf16[128,16,256]{2,1,0:T(8,128)(2,1)} fusion(bf16[1024,16,256]{2,1,0:T(8,128)(2,1)} %param.12, s32[1024]{0:T(1024)S(1)} %pad_clamp_fusion), kind=kCustom, calls=%fused_computation | custom fusion | bytes 2097664 | tf_op jit(solution)/shard_map/gather | solution.py:44
  14.6 7.1 %all-to-all-start = ((bf16[16,8,16,256]{3,2,1,0:T(8,128)(2,1)}), bf16[16,8,16,256]{3,2,1,0:T(8,128)(2,1)S(1)}, u32[]{:S(2)}, u32[]{:S(2)}) async-start(bf16[16,8,16,256]{3,2,1,0:T(8,128)(2,1)} %bitcast.1), calls=%async_computation | async-start | bytes 2097152 | tf_op jit(solution)/shard_map/all_to_all | solution.py:45
  21.7 0.0 reduce-scatter.2.cloned.1.call-start
  21.8 0.7 convert_element_type.36
  22.4 0.7 compare_select_fusion
  23.1 0.1 copy.17
  23.2 0.1 reshape.232
  23.4 0.7 iota_compare_fusion
  24.1 0.3 multiply_cosine_fusion.1
  24.4 14.4 %all-to-all-done = bf16[16,8,16,256]{3,2,1,0:T(8,128)(2,1)S(1)} async-done(((bf16[16,8,16,256]{3,2,1,0:T(8,128)(2,1)}), bf16[16,8,16,256]{3,2,1,0:T(8,128)(2,1)S(1)}, u32[]{:S(2)}, u32[]{:S(2)}) %all-to-all-start) | async-done | bytes 1048608 | tf_op jit(solution)/shard_map/all_to_all | solution.py:45
  38.9 10.3 %pad_maximum_fusion = bf16[1152,16,256]{2,1,0:T(8,128)(2,1)} fusion(bf16[128,16,256]{2,1,0:T(8,128)(2,1)S(1)} %bitcast.103, bf16[1024,16,256]{2,1,0:T(8,128)(2,1)} %param.12), kind=kLoop, calls=%fused_computation.3 | loop fusion | flops 4718592 | bytes 18874368 | tf_op jit(solution)/shard_map/concatenate | solution.py:46
  49.2 13.7 %gather_fusion.1 = bf16[1024,16,256]{2,1,0:T(8,128)(2,1)} fusion(bf16[1152,16,256]{2,1,0:T(8,128)(2,1)} %pad_maximum_fusion, s32[1024]{0:T(1024)S(1)} %broadcast_clamp_fusion), kind=kCustom, calls=%fused_computation.1 | custom fusion | bytes 16781312 | tf_op jit(solution)/shard_map/gather | solution.py:48
  62.9 12.6 %reshape.215 = bf16[128,128,1,2,128]{4,3,1,0,2:T(2,128)(2,1)} reshape(bf16[1024,16,256]{2,1,0:T(8,128)(2,1)} %gather_fusion.1) | data formatting | bytes 16777216 | tf_op jit(solution)/shard_map/reshape | solution.py:48
  75.5 20.1 %fusion.39 = (bf16[128,128,1,1,128]{4,3,1,0,2:T(2,128)(2,1)}, bf16[128,128,1,1,128]{4,3,1,0,2:T(2,128)(2,1)}) fusion(bf16[128,128,1,2,128]{4,3,1,0,2:T(2,128)(2,1)} %reshape.215), kind=kLoop, calls=%fused_computation.64 | loop fusion | bytes 16777216 | tf_op jit(solution)/shard_map/slice | solution.py:49
  95.7 0.0 all-gather.6.cloned.1.call-done
  95.7 6.4 %copy.22 = bf16[256,8192]{1,0:T(8,128)(2,1)} copy(bf16[256,8192]{0,1:T(8,128)(2,1)} %bitcast.104) | data formatting | bytes 8388608 | tf_op jit(solution)/shard_map/dot_general | solution.py:33
  102.1 4.8 %fusion.12 = f32[2,128,1,2,128]{1,4,3,0,2:T(8,128)S(1)} fusion(bf16[2,128,8192,1]{2,1,0,3:T(8,128)(2,1)} %bitcast.105, bf16[2,128,8192]{2,1,0:T(8,128)(2,1)} %param.8), kind=kOutput, calls=%fused_computation.20 | convolution fusion | flops 1073741824 | bytes 8650752 | tf_op jit(solution)/shard_map/dot_general | solution.py:33
  106.9 0.3 fusion.38
  107.2 0.1 copy.29
  107.4 0.1 copy.31
  107.5 73.8 %all-gather.4.cloned.1.call-done = bf16[8192,1024]{1,0:T(8,128)(2,1)} async-done(((bf16[512,1024]{1,0:T(8,128)(2,1)}), bf16[8192,1024]{1,0:T(8,128)(2,1)}) %all-gather.4.cloned.1.call-update) | async-done | bytes 16777232 | tf_op jit(solution)/shard_map/all_gather | solution.py:35
  181.3 21.5 %copy.20 = bf16[1024,8192]{1,0:T(8,128)(2,1)} copy(bf16[1024,8192]{0,1:T(8,128)(2,1)} %bitcast.101) | data formatting | bytes 33554432 | tf_op jit(solution)/shard_map/dot_general | solution.py:33
  202.7 10.0 %fusion.4 = f32[2,128,8,128]{1,3,2,0:T(8,128)S(1)} fusion(bf16[8,128,8192,1]{2,1,0,3:T(8,128)(2,1)} %bitcast.102, bf16[2,128,8192]{2,1,0:T(8,128)(2,1)} %param.8), kind=kOutput, calls=%fused_computation.10 | convolution fusion | flops 4294967296 | bytes 22020096 | tf_op jit(solution)/shard_map/dot_general | solution.py:33
  212.7 0.2 subtract_convert_fusion
  212.9 0.4 copy.21
  213.4 2.5 fusion.41
  215.8 5.9 %fusion.40 = (f32[2,128,8]{2,0,1:T(2,128)S(1)}, f32[2,128,1,8,128]{4,3,0,1,2:T(8,128)S(1)}) fusion(bf16[2,128,8,128]{3,2,0,1:T(8,128)(2,1)S(1)} %copy.21, bf16[128,128,1,1,128]{4,3,1,0,2:T(2,128)(2,1)} %get-tuple-element.5, pred[128,128]{1,0:T(8,128)(4,1)S(1)} %iota_compare_fusion), kind=kOutput, calls=%fused_computation.65 | convolution fusion | flops 67893248 | bytes 5791744 | tf_op jit(solution)/shard_map/trkgd,rckd->trkgc/dot_general | solution.py:54
  221.7 0.1 max.9
  221.8 0.5 fusion.23
  222.3 0.8 fusion.16
  223.1 0.1 add.74
  223.2 4.6 %fusion.1 = f32[128,128,2,8]{1,3,2,0:T(8,128)S(1)} fusion(bf16[128,128,1,1,128]{4,3,1,0,2:T(2,128)(2,1)} %get-tuple-element.6, f32[2,128,1,8,128]{4,3,0,1,2:T(8,128)S(1)} %get-tuple-element.14, f32[2,128,8]{2,0,1:T(2,128)S(1)} %max.9), kind=kOutput, calls=%fused_computation.7 | convolution fusion | flops 67633152 | bytes 6299648 | tf_op jit(solution)/shard_map/trkgc,rckd->trkgd/dot_general | solution.py:69
  227.8 0.6 divide_convert_fusion
  228.5 71.6 %all-gather.8.cloned.1.call-done = bf16[1024,8192]{1,0:T(8,128)(2,1)} async-done(((bf16[1024,512]{1,0:T(8,128)(2,1)}), bf16[1024,8192]{1,0:T(8,128)(2,1)}) %all-gather.8.cloned.1.call-update) | async-done | bytes 16777232 | tf_op jit(solution)/shard_map/all_gather | solution.py:85
  300.1 11.8 %convolution_convert_fusion = bf16[256,8192]{1,0:T(8,128)(2,1)} fusion(bf16[1024,8192]{1,0:T(8,128)(2,1)} %all-gather.8.cloned.1.call-done, bf16[32,8,8,128]{3,2,1,0:T(8,128)(2,1)S(1)} %bitcast.106), kind=kOutput, calls=%fused_computation.2 | convolution fusion | flops 4297064448 | bytes 21495808 | tf_op jit(solution)/shard_map/dot_general | solution.py:83
  311.9 0.0 reduce-scatter.2.cloned.1.call-update
  311.9 91.4 %reduce-scatter.2.cloned.1.call-done = bf16[256,1024]{1,0:T(8,128)(2,1)} async-done(((bf16[256,8192]{1,0:T(8,128)(2,1)}), bf16[256,1024]{1,0:T(8,128)(2,1)}) %reduce-scatter.2.cloned.1.call-update) | async-done | bytes 524304 | tf_op jit(solution)/shard_map/reduce_scatter | solution.py:89
  (10 shorter events, 0.1 us)
Async XLA Ops:
  6.5 89.2 %all-gather.6.cloned.1.call-start = ((), (), s32[]{:S(2)}) async-start(), calls=%async_computation.3 | async-start | bytes 4456448 | tf_op jit(solution)/shard_map/all_gather | solution.py:36
  7.3 174.0 %all-gather.4.cloned.1.call-start = ((), (), s32[]{:S(2)}) async-start(), calls=%async_computation.2 | async-start | bytes 17825792 | tf_op jit(solution)/shard_map/all_gather | solution.py:35
  8.0 292.1 %all-gather.8.cloned.1.call-start = ((), (), s32[]{:S(2)}) async-start(), calls=%async_computation.4 | async-start | bytes 17825792 | tf_op jit(solution)/shard_map/all_gather | solution.py:85
  14.6 24.3 %all-to-all-start = ((bf16[16,8,16,256]{3,2,1,0:T(8,128)(2,1)}), bf16[16,8,16,256]{3,2,1,0:T(8,128)(2,1)S(1)}, u32[]{:S(2)}, u32[]{:S(2)}) async-start(bf16[16,8,16,256]{3,2,1,0:T(8,128)(2,1)} %bitcast.1), calls=%async_computation | async-start | bytes 2097152 | tf_op jit(solution)/shard_map/all_to_all | solution.py:45
  21.7 381.7 %reduce-scatter.2.cloned.1.call-start = ((), (), s32[]{:S(2)}) async-start(), calls=%async_computation.5 | async-start | bytes 4718592 | tf_op jit(solution)/shard_map/reduce_scatter | solution.py:89
Sparse Core Ops, SparseCore 0:
  9.8 62.1 all-gather.5
  74.5 106.6 all-gather.3
  183.5 116.5 all-gather.7
  312.1 91.2 reduce-scatter.1
where the time goes:
time: 413 us; the launch traced here: 410 us
  waiting for transfers between devices  253 us (61%)
  local copies, waits for them, and re-layouts  80.4 us (19%)
  matrix products  40.2 us (10%)
  other arithmetic  15.4 us (4%)
  between operations  13.3 us (3%)
  starting transfers between devices  7.23 us (2%)
    reduce_scatter x1, waiting for transfers between devices, per_device(): lax.psum_scatter(partial_term.astype(jnp.bfloat16), 'mp', scatter_dimensi...  91.4 us
    all_gather x1, waiting for transfers between devices, per_device(): query = add_rows(lax.all_gather(q_weight, 'group', axis=0, tiled=True))  73.8 us
    all_gather x1, waiting for transfers between devices, per_device(): lax.all_gather(o_weight, 'group', axis=1, tiled=True)  71.6 us
    dot_general x2, local copies, waits for them, and re-layouts, add_rows(): return jnp.dot(flat, piece, preferred_element_type=jnp.float32)  27.9 us
    slice x1, local copies, waits for them, and re-layouts, per_device(): key_cache = cache[:, :, :, 0]  20.1 us
    dot_general x2, matrix products, add_rows(): return jnp.dot(flat, piece, preferred_element_type=jnp.float32)  14.8 us
    all_to_all x1, waiting for transfers between devices, per_device(): lax.all_to_all(outgoing, 'group', split_axis=0, concat_axis=0, tiled=True)  14.4 us
    gather x1, local copies, waits for them, and re-layouts, per_device(): cache = held[page_table].reshape(rows, context, kv_here, 2, HD)  13.7 us
  transfers between devices with their start and end apart: 5, of which 4 were waited for; matrix products, arithmetic and copies ran while one was open for 30% of the time, Pallas kernels for 0%

commit v1 on v0

v1 whole, which is shorter than its diff:
```python
import jax
import jax.numpy as jnp
from jax import lax
from jax.experimental import pallas as pl
from jax.experimental.pallas import tpu as pltpu
from jax.sharding import PartitionSpec as P

HD = 128
MESH = pl.DeviceIdType.MESH
BF16 = jnp.bfloat16
F32 = jnp.float32

Q_UP, Q_DN, Q_FUP, Q_FDN, Q_SIB = 0, 2, 4, 5, 6
T_X, T_Z, P_X = 11, 12, 15
O_X, O_UP, O_DN, O_FUP, O_FDN, O_SIB = 16, 17, 21, 25, 27, 29
R_X = 39
N_REMOTE = 40


def kernel(
    tokens, q_weight, kv_weight, o_weight, pool, cos, sin, send_list, table, lengths, out,
    wq, wo, tok, held, arrived, outgoing, acc, psend, precv, q3, k_new, v_new, attn,
    part, zrecv, xsend, xrecv,
    ssem, rsem, page_ssem, page_rsem, z_ssem, z_rsem, lsem,
):
    g = lax.axis_index("group")
    m = lax.axis_index("mp")
    xh, y, c = g // 8, (g // 2) % 4, g % 2
    z, xl = m // 2, m % 2
    up, dn, opp = (y + 1) % 4, (y + 3) % 4, (y + 2) % 4

    def in_group(xh_, y_, c_):
        return (xh_ * 8 + y_ * 2 + c_, m)

    to_up, to_dn = in_group(xh, up, c), in_group(xh, dn, c)
    to_x, to_sib = in_group(1 - xh, y, c), in_group(xh, y, 1 - c)

    def remote(src, dst, number, device):
        return pltpu.make_async_remote_copy(
            src_ref=src, dst_ref=dst, send_sem=ssem.at[number], recv_sem=rsem.at[number],
            device_id=device, device_id_type=MESH,
        )

    half = pl.multiple_of(xh * 4096, 4096)
    other_half = pl.multiple_of((1 - xh) * 4096, 4096)
    my_rows = pl.ds(pl.multiple_of(c * 512, 512), 512)
    my_cols = pl.ds(pl.multiple_of(c * 512, 512), 512)
    own_chip = xh * 4 + y
    loads = [
        pltpu.make_async_copy(q_weight, wq.at[y, my_rows, pl.ds(0, 1024)], lsem.at[0]),
        pltpu.make_async_copy(kv_weight, wq.at[y, my_rows, pl.ds(1024, 256)], lsem.at[1]),
        pltpu.make_async_copy(o_weight, wo.at[own_chip, :, my_cols], lsem.at[2]),
        pltpu.make_async_copy(pool, held.at[pl.ds(0, 1024)], lsem.at[3]),
        pltpu.make_async_copy(tokens.at[:, pl.ds(half, 4096)], tok.at[0], lsem.at[4]),
    ]
    for load in loads:
        load.start()

    barrier = pltpu.get_barrier_semaphore()
    for off in range(1, 16):
        pl.semaphore_signal(barrier, inc=1, device_id=((g + off) % 16, m), device_id_type=MESH)
    for off in range(1, 4):
        pl.semaphore_signal(
            barrier, inc=1, device_id=(g, ((z + off) % 4) * 2 + xl), device_id_type=MESH
        )
    to_lo = (g, z * 2 + 1 - xl)
    pl.semaphore_signal(barrier, inc=1, device_id=to_lo, device_id_type=MESH)
    pl.semaphore_wait(barrier, 19)

    sent = []

    def start(copy):
        copy.start()
        sent.append(copy)
        return copy

    my_quarter = pl.ds(pl.multiple_of(z * 64, 64), 64)
    t_x = start(remote(
        tokens.at[my_quarter, pl.ds(other_half, 4096)], tok.at[1, my_quarter], T_X, to_x))

    def q_piece(yy, h):
        return wq.at[yy, pl.ds(pl.multiple_of(c * 512 + h * 256, 256), 256)]

    def q_block(yy):
        return wq.at[yy, my_rows]

    loads[0].wait()
    loads[1].wait()
    q_up, q_dn = [None, None], [None, None]
    for h in (0, 1):
        q_up[h] = start(remote(q_piece(y, h), q_piece(y, h), Q_UP + h, to_up))
        q_dn[1 - h] = start(remote(q_piece(y, 1 - h), q_piece(y, 1 - h), Q_DN + 1 - h, to_dn))
    q_sib = [start(remote(q_block(y), q_block(y), Q_SIB, to_sib))]

    def o_block(chip):
        return wo.at[chip, :, my_cols]

    def o_piece(chip, h):
        return wo.at[chip, pl.ds(h * 512, 512), my_cols]

    loads[2].wait()
    o_x = start(remote(o_block(own_chip), o_block(own_chip), O_X, to_x))
    o_sib = [start(remote(o_block(own_chip), o_block(own_chip), O_SIB, to_sib))]

    loads[3].wait()

    def gather_page(i, carry):
        outgoing[i] = held[send_list[i]]
        return carry

    lax.fori_loop(0, 128, gather_page, 0)

    t_x.wait_recv()
    t_z = []
    for off in range(1, 4):
        t_z.append(start(remote(
            tok.at[1, my_quarter], tok.at[1, my_quarter], T_Z + off - 1,
            (g, ((z + off) % 4) * 2 + xl))))

    def project(which, yy, first):
        left = pl.ds(pl.multiple_of(yy * 1024, 1024), 1024)

        def step(n, carry):
            cols = pl.ds(pl.multiple_of(n * 256, 256), 256)
            product = jnp.dot(
                tok[which, :, left], wq[yy, :, cols], preferred_element_type=F32)
            acc[which, :, cols] = product if first else acc[which, :, cols] + product
            return carry

        lax.fori_loop(0, 5, step, 0)

    q_up[0].wait_recv()
    q_fup = start(remote(q_piece(dn, 0), q_piece(dn, 0), Q_FUP, to_up))
    q_dn[1].wait_recv()
    q_fdn = start(remote(q_piece(up, 1), q_piece(up, 1), Q_FDN, to_dn))

    loads[4].wait()
    q_sib[0].wait_recv()
    project(0, y, True)

    q_up[1].wait_recv()
    q_sib.append(start(remote(q_block(dn), q_block(dn), Q_SIB + 1, to_sib)))
    q_dn[0].wait_recv()
    q_sib.append(start(remote(q_block(up), q_block(up), Q_SIB + 2, to_sib)))
    q_sib[1].wait_recv()
    project(0, dn, False)
    q_sib[2].wait_recv()
    project(0, up, False)

    for copy in t_z:
        copy.wait_recv()
    project(1, y, True)
    project(1, dn, False)
    project(1, up, False)

    q_fup.wait_recv()
    q_sib.append(start(remote(q_piece(opp, 0), q_piece(opp, 0), Q_SIB + 3, to_sib)))
    q_fdn.wait_recv()
    q_sib.append(start(remote(q_piece(opp, 1), q_piece(opp, 1), Q_SIB + 4, to_sib)))

    pages = []
    for off in range(1, 16):
        there = (g + off) % 16
        copy = pltpu.make_async_remote_copy(
            src_ref=outgoing.at[pl.ds(there * 8, 8)], dst_ref=arrived.at[pl.ds(g * 8, 8)],
            send_sem=page_ssem.at[off - 1], recv_sem=page_rsem.at[off - 1],
            device_id=(there, m), device_id_type=MESH)
        copy.start()
        pages.append(copy)
        sent.append(copy)
    own_pages = pltpu.make_async_copy(
        outgoing.at[pl.ds(g * 8, 8)], arrived.at[pl.ds(g * 8, 8)], lsem.at[5])
    own_pages.start()

    o_x.wait_recv()
    partner_chip = (1 - xh) * 4 + y
    o_sib.append(start(remote(o_block(partner_chip), o_block(partner_chip), O_SIB + 1, to_sib)))
    o_up, o_dn = [[None, None], [None, None]], [[None, None], [None, None]]
    for k, chip in enumerate((own_chip, partner_chip)):
        for h in (0, 1):
            o_up[k][h] = start(remote(
                o_piece(chip, h), o_piece(chip, h), O_UP + 2 * k + h, to_up))
            o_dn[k][1 - h] = start(remote(
                o_piece(chip, 1 - h), o_piece(chip, 1 - h), O_DN + 2 * k + 1 - h, to_dn))

    q_sib[3].wait_recv()
    q_sib[4].wait_recv()
    project(1, opp, False)
    psend[...] = acc[1].astype(BF16)
    p_x = start(remote(psend, precv, P_X, to_x))
    project(0, opp, False)

    for copy in pages:
        copy.wait_recv()
    own_pages.wait()
    append = pltpu.make_async_copy(arrived, held.at[pl.ds(1024, 128)], lsem.at[6])
    append.start()

    p_x.wait_recv()
    for t in range(2):
        rows = pl.ds(t * 128, 128)

        def whole(first):
            cols = pl.ds(first, HD)
            return acc[0, rows, cols] + precv[rows, cols].astype(F32)

        def rotated(value):
            turned = jnp.concatenate([value[:, 64:], value[:, :64]], axis=1)
            value = value * cos[rows, :] + turned * sin[rows, :]
            return value.astype(BF16).astype(F32)

        for h in range(8):
            q3[:, t * 8 + h, :] = rotated(whole(h * HD))
        k_new[rows, :] = rotated(whole(1024))
        v_new[rows, :] = whole(1024 + HD).astype(BF16).astype(F32)
    append.wait()

    scale = 1.0 / HD**0.5
    position = lax.broadcasted_iota(jnp.int32, (16, 128), 1)
    second = lax.broadcasted_iota(jnp.int32, (16, 1), 0) >= 8

    def attend(i, carry):
        for k in range(8):
            r = i * 8 + k
            cache = jnp.concatenate([held[table[r * 8 + j]] for j in range(8)], axis=0)
            query = q3[r]
            scores = lax.dot_general(
                query.astype(BF16), cache[:, :HD], (((1,), (1,)), ((), ())),
                preferred_element_type=F32) * scale
            scores = jnp.where(position < lengths[r], scores, -jnp.inf)
            new0 = jnp.sum(query * k_new[pl.ds(r, 1), :], axis=1, keepdims=True) * scale
            new1 = jnp.sum(query * k_new[pl.ds(128 + r, 1), :], axis=1, keepdims=True) * scale
            new1 = jnp.where(second, new1, -jnp.inf)
            top = jnp.maximum(
                jnp.max(scores, axis=1, keepdims=True), jnp.maximum(new0, new1))
            weights = jnp.exp(scores - top)
            weight0 = jnp.exp(new0 - top)
            weight1 = jnp.exp(new1 - top)
            total = jnp.sum(weights, axis=1, keepdims=True) + weight0 + weight1
            numer = jnp.dot(
                weights.astype(BF16), cache[:, HD:], preferred_element_type=F32)
            numer = numer + weight0.astype(BF16).astype(F32) * v_new[pl.ds(r, 1), :]
            numer = numer + weight1.astype(BF16).astype(F32) * v_new[pl.ds(128 + r, 1), :]
            q3[r] = numer / total
        return carry

    lax.fori_loop(0, 16, attend, 0)
    for t in range(2):
        for h in range(8):
            attn[pl.ds(t * 128, 128), pl.ds(h * HD, HD)] = q3[:, t * 8 + h, :].astype(BF16)

    def z_copy(chip):
        there = chip // 2
        slot = (z - there + 4) % 4 - 1
        return pltpu.make_async_remote_copy(
            src_ref=part.at[chip], dst_ref=zrecv.at[slot, chip % 2],
            send_sem=z_ssem.at[chip], recv_sem=z_rsem.at[slot, chip % 2],
            device_id=(g, there * 2 + xl), device_id_type=MESH)

    def unit(chip):
        def step(n, carry):
            cols = pl.ds(pl.multiple_of(n * 256, 256), 256)
            part[chip, :, cols] = jnp.dot(
                attn[...], wo[chip, :, cols], preferred_element_type=F32).astype(BF16)
            return carry

        lax.fori_loop(0, 4, step, 0)

        @pl.when(chip // 2 != z)
        def _():
            z_copy(chip).start()

    o_sib[0].wait_recv()
    unit(own_chip)
    o_sib[1].wait_recv()
    unit(partner_chip)
    o_fup, o_fdn = [], []
    for k, side in enumerate((xh, 1 - xh)):
        o_up[k][0].wait_recv()
        o_fup.append(start(remote(
            o_piece(side * 4 + dn, 0), o_piece(side * 4 + dn, 0), O_FUP + k, to_up)))
        o_dn[k][1].wait_recv()
        o_fdn.append(start(remote(
            o_piece(side * 4 + up, 1), o_piece(side * 4 + up, 1), O_FDN + k, to_dn)))
        o_up[k][1].wait_recv()
        o_sib.append(start(remote(
            o_block(side * 4 + dn), o_block(side * 4 + dn), O_SIB + 2 + 2 * k, to_sib)))
        o_dn[k][0].wait_recv()
        o_sib.append(start(remote(
            o_block(side * 4 + up), o_block(side * 4 + up), O_SIB + 3 + 2 * k, to_sib)))
        o_sib[2 + 2 * k].wait_recv()
        unit(side * 4 + dn)
        o_sib[3 + 2 * k].wait_recv()
        unit(side * 4 + up)
    for k, side in enumerate((xh, 1 - xh)):
        o_fup[k].wait_recv()
        o_sib.append(start(remote(
            o_piece(side * 4 + opp, 0), o_piece(side * 4 + opp, 0), O_SIB + 6 + 2 * k, to_sib)))
        o_fdn[k].wait_recv()
        o_sib.append(start(remote(
            o_piece(side * 4 + opp, 1), o_piece(side * 4 + opp, 1), O_SIB + 7 + 2 * k, to_sib)))
        o_sib[6 + 2 * k].wait_recv()
        o_sib[7 + 2 * k].wait_recv()
        unit(side * 4 + opp)

    def z_sum(lo, cols):
        total = part[z * 2 + lo, :, cols].astype(F32)
        for slot in range(3):
            total = total + zrecv[slot, lo, :, cols].astype(F32)
        return total

    def z_wait(lo):
        for slot in range(3):
            pltpu.make_async_copy(
                zrecv.at[slot, lo], zrecv.at[slot, lo], z_rsem.at[slot, lo]).wait()

    z_wait(1 - xl)

    def sum_other(n, carry):
        cols = pl.ds(pl.multiple_of(n * 256, 256), 256)
        xsend[:, cols] = z_sum(1 - xl, cols).astype(BF16)
        return carry

    lax.fori_loop(0, 4, sum_other, 0)
    r_x = start(remote(xsend, xrecv, R_X, to_lo))
    z_wait(xl)
    r_x.wait_recv()

    def sum_own(n, carry):
        cols = pl.ds(pl.multiple_of(n * 256, 256), 256)
        out[:, cols] = (z_sum(xl, cols) + xrecv[:, cols].astype(F32)).astype(BF16)
        return carry

    lax.fori_loop(0, 4, sum_own, 0)

    for copy in sent:
        copy.wait_send()
    for chip in range(8):
        @pl.when(chip // 2 != z)
        def _():
            z_copy(chip).wait_send()


def per_device(tokens, q_weight, kv_weight, o_weight, kv_pool, send_list, page_table, lengths):
    rows = tokens.shape[1]
    flat = tokens.reshape(2 * rows, tokens.shape[2])
    inverse = 500000.0 ** (-(jnp.arange(64, dtype=F32) * 2.0) / 128.0)
    position = (lengths[None, :].astype(F32) + jnp.arange(2, dtype=F32)[:, None]).reshape(-1)
    angle = position[:, None] * inverse
    cosine, sine = jnp.cos(angle), jnp.sin(angle)
    cos = jnp.concatenate([cosine, cosine], axis=1)
    sin = jnp.concatenate([-sine, sine], axis=1)
    hbm = pl.BlockSpec(memory_space=pl.ANY)
    vmem = pl.BlockSpec(memory_space=pltpu.VMEM)
    smem = pl.BlockSpec(memory_space=pltpu.SMEM)
    mixed = pl.pallas_call(
        kernel,
        out_shape=jax.ShapeDtypeStruct((256, 1024), BF16),
        in_specs=[hbm] * 5 + [vmem] * 2 + [smem] * 3,
        out_specs=vmem,
        scratch_shapes=[
            pltpu.VMEM((4, 1024, 1280), BF16),
            pltpu.VMEM((8, 1024, 1024), BF16),
            pltpu.VMEM((2, 256, 4096), BF16),
            pltpu.VMEM((1152, 16, 256), BF16),
            pltpu.VMEM((128, 16, 256), BF16),
            pltpu.VMEM((128, 16, 256), BF16),
            pltpu.VMEM((2, 256, 1280), F32),
            pltpu.VMEM((256, 1280), BF16),
            pltpu.VMEM((256, 1280), BF16),
            pltpu.VMEM((128, 16, 128), F32),
            pltpu.VMEM((256, 128), F32),
            pltpu.VMEM((256, 128), F32),
            pltpu.VMEM((256, 1024), BF16),
            pltpu.VMEM((8, 256, 1024), BF16),
            pltpu.VMEM((3, 2, 256, 1024), BF16),
            pltpu.VMEM((256, 1024), BF16),
            pltpu.VMEM((256, 1024), BF16),
            pltpu.SemaphoreType.DMA((N_REMOTE,)),
            pltpu.SemaphoreType.DMA((N_REMOTE,)),
            pltpu.SemaphoreType.DMA((15,)),
            pltpu.SemaphoreType.DMA((15,)),
            pltpu.SemaphoreType.DMA((8,)),
            pltpu.SemaphoreType.DMA((3, 2)),
            pltpu.SemaphoreType.DMA((7,)),
        ],
        compiler_params=pltpu.CompilerParams(
            collective_id=0, has_side_effects=True, vmem_limit_bytes=60 * 2**20),
    )(
        flat, q_weight, kv_weight, o_weight, kv_pool, cos, sin,
        send_list.reshape(-1), page_table.reshape(-1), lengths,
    )
    return mixed.reshape(2, rows, -1)


def solution(mesh):
    in_specs = (
        P(None, "group", None),
        P("group", "mp"),
        P("group", "mp"),
        P("mp", "group"),
        P("group", None, "mp"),
        P("group", None, None),
        P("group", None),
        P("group"),
    )
    out_specs = P(None, "group", "mp")
    return jax.shard_map(
        per_device, mesh=mesh, in_specs=in_specs, out_specs=out_specs, check_vma=False
    )
```

time: 413 us -> 195 us (0.47)
  waiting for transfers between devices: 253 us -> 0 us
  Pallas kernels: 0 us -> 188 us
  local copies, waits for them, and re-layouts: 80.4 us -> 4.7 us
  matrix products: 40.2 us -> 0 us
  other arithmetic: 15.4 us -> 2.05 us
  between operations: 13.3 us -> 0.02 us
  starting transfers between devices: 7.23 us -> 0 us
    pallas_call x0 -> x1, Pallas kernels: none -> 188 us  [per_device(): pl.pallas_call(kernel, out_shape=jax.ShapeDtypeStruct((256, 1024), BF16),...]
    all_gather x3 -> x0, waiting for transfers between devices: 145 us -> none  [the longest x1 73.8 us: per_device(): query = add_rows(lax.all_gather(q_weight, 'group', axis=0, tiled=True))]
    reduce_scatter x1 -> x0, waiting for transfers between devices: 91.4 us -> none  [per_device(): lax.psum_scatter(partial_term.astype(jnp.bfloat16), 'mp', scatter_dimensi...]
    dot_general x7 -> x0, matrix products: 40.2 us -> none  [the longest x2 14.8 us: add_rows(): return jnp.dot(flat, piece, preferred_element_type=jnp.float32)]
    dot_general x2 -> x0, local copies, waits for them, and re-layouts: 27.9 us -> none  [add_rows(): return jnp.dot(flat, piece, preferred_element_type=jnp.float32)]
    slice x1 -> x0, local copies, waits for them, and re-layouts: 20.1 us -> none  [per_device(): key_cache = cache[:, :, :, 0]]
    gather x2 -> x0, local copies, waits for them, and re-layouts: 18.7 us -> none  [the longest x1 13.7 us: per_device(): cache = held[page_table].reshape(rows, context, kv_here, 2, HD)]
    all_to_all x1 -> x0, waiting for transfers between devices: 14.4 us -> none  [per_device(): lax.all_to_all(outgoing, 'group', split_axis=0, concat_axis=0, tiled=True)]
  transfers between devices with their start and end apart: 5 -> 0, of which waited for: 4 -> 0; matrix products, arithmetic and copies ran while one was open for 30% -> 0% of each run, Pallas kernels for 0% -> 0%
where the time goes in v1:
time: 195 us
  Pallas kernels  188 us (96%)
  local copies, waits for them, and re-layouts  4.7 us (2%)
  other arithmetic  2.05 us (1%)
    pallas_call x1, Pallas kernels, per_device(): pl.pallas_call(kernel, out_shape=jax.ShapeDtypeStruct((256, 1024), BF16),...  188 us

profile of v1, /device:TPU:30, one launch (start us, length us, event | category | flops | bytes accessed | tf_op | source)
XLA Modules:
  0.0 195.1 jit_solution(2266063553575743810)
XLA Ops:
  0.0 0.7 convert_element_type.4
  0.7 0.8 copy.10
  1.4 0.6 reshape.36.send_list
  2.1 0.8 copy.11
  2.8 0.7 reshape.37.table
  3.5 0.5 fusion
  4.0 0.8 pad_maximum_fusion
  4.9 188.3 %shard_map.82 = bf16[256,1024]{1,0:T(8,128)(2,1)} custom-call(bf16[256,8192]{1,0:T(8,128)(2,1)} %bitcast.4, bf16[512,1024]{1,0:T(8,128)(2,1)} %q_weight.1, bf16[512,256]{1,0:T(8,128)(2,1)} %kv_weight.1, bf16[1024,512]{1,0:T(8,128)(2,1)} %o_weight.1, bf16[1024,16,256]{2,1,0:T(8,128)(2,1)} %pool.1, f32[256,128]{1,0:T(8,128)} %get-tuple-element.8.cos, ...), custom_call_target="tpu_custom_call" | custom-call | tf_op jit(solution)/shard_map/pallas_call | solution.py:356
  193.2 1.9 copy.13
  (2 shorter events, 0.0 us)

commit v2 on v0

v2 whole, which is shorter than its diff:
```python
import jax
import jax.numpy as jnp
from jax import lax
from jax.experimental import pallas as pl
from jax.experimental.pallas import tpu as pltpu
from jax.sharding import PartitionSpec as P

HD = 128
GROUP = 16
MESH = pl.DeviceIdType.MESH
BF16 = jnp.bfloat16
F32 = jnp.float32
LOG_BASE = 13.122363377404328

Q_UP, Q_DN, Q_FUP, Q_FDN, Q_SIB = 0, 2, 4, 5, 6
T_X, T_Z, P_X, G_X, G_Y = 11, 12, 15, 16, 17
B_UP, B_DN, B_FUP, B_FDN, B_X, B_SIB = 24, 26, 28, 29, 30, 35
A_X, A_UP, A_DN, A_FUP, A_FDN, A_SIB = 45, 46, 50, 54, 56, 58
R_X = 68
N_REMOTE = 82
WIDTH = (768, 512)


def kernel(
    tokens, q_weight, kv_weight, o_weight, pool, row_lengths, send_list, table, lengths, out,
    wq0, wq1, wo, tok, held, arrived, leaving, staying, acc0, acc1, psend0, psend1, precv0, precv1, q3, k_new, v_new, attn,
    part, zmid, zrecv, xsend, xrecv,
    ssem, rsem, z_ssem, mid_rsem, z_rsem, lsem,
):
    g = lax.axis_index("group")
    m = lax.axis_index("mp")
    wq, acc, psend, precv = (wq0, wq1), (acc0, acc1), (psend0, psend1), (precv0, precv1)
    xh, y, c = g // 8, (g // 2) % 4, g % 2
    z, xl = m // 2, m % 2
    up, dn, opp = (y + 1) % 4, (y + 3) % 4, (y + 2) % 4
    z_up, z_dn = (z + 1) % 4, (z + 3) % 4
    me = y * 2 + c

    def in_group(xh_, y_, c_):
        return (xh_ * 8 + y_ * 2 + c_, m)

    to_up, to_dn = in_group(xh, up, c), in_group(xh, dn, c)
    to_x, to_sib = in_group(1 - xh, y, c), in_group(xh, y, 1 - c)
    to_lo = (g, z * 2 + 1 - xl)

    def at_z(z_):
        return (g, z_ * 2 + xl)

    half = pl.multiple_of(xh * 4096, 4096)
    other_half = pl.multiple_of((1 - xh) * 4096, 4096)
    my_rows = pl.ds(pl.multiple_of(c * 512, 512), 512)
    my_cols = pl.ds(pl.multiple_of(c * 256, 256), 256)
    own_chip, partner_chip = xh * 4 + y, (1 - xh) * 4 + y
    loads = [
        pltpu.make_async_copy(kv_weight, wq0.at[y, my_rows, pl.ds(0, 256)], lsem.at[0]),
        pltpu.make_async_copy(
            q_weight.at[:, pl.ds(0, 512)], wq0.at[y, my_rows, pl.ds(256, 512)], lsem.at[1]),
        pltpu.make_async_copy(q_weight.at[:, pl.ds(512, 512)], wq1.at[y, my_rows], lsem.at[9]),
        pltpu.make_async_copy(pool, held.at[pl.ds(0, 1024)], lsem.at[2]),
        pltpu.make_async_copy(
            o_weight.at[:, pl.ds(256, 256)], wo.at[1, own_chip, :, my_cols], lsem.at[3]),
        pltpu.make_async_copy(
            o_weight.at[:, pl.ds(0, 256)], wo.at[0, own_chip, :, my_cols], lsem.at[4]),
        pltpu.make_async_copy(tokens.at[:, pl.ds(half, 4096)], tok.at[0], lsem.at[5]),
    ]
    for load in loads:
        load.start()

    barrier = pltpu.get_barrier_semaphore()
    for off in range(1, 8):
        pl.semaphore_signal(
            barrier, inc=1, device_id=(xh * 8 + (me + off) % 8, m), device_id_type=MESH)
    for off in range(1, 4):
        pl.semaphore_signal(barrier, inc=1, device_id=at_z((z + off) % 4), device_id_type=MESH)
    pl.semaphore_signal(barrier, inc=1, device_id=to_x, device_id_type=MESH)
    pl.semaphore_signal(barrier, inc=1, device_id=to_lo, device_id_type=MESH)
    pl.semaphore_wait(barrier, 12)

    sent = []

    def send(ref, number, device, there=None):
        copy = pltpu.make_async_remote_copy(
            src_ref=ref, dst_ref=ref if there is None else there,
            send_sem=ssem.at[number], recv_sem=rsem.at[number],
            device_id=device, device_id_type=MESH,
        )
        copy.start()
        sent.append(copy)
        return copy

    my_quarter = pl.ds(pl.multiple_of(z * 64, 64), 64)
    t_x = send(
        tokens.at[my_quarter, pl.ds(other_half, 4096)], T_X, to_x, tok.at[1, my_quarter])

    def q_piece(part, yy, h):
        return wq[part].at[yy, pl.ds(pl.multiple_of(c * 512 + h * 256, 256), 256)]

    def q_block(part, yy):
        return wq[part].at[yy, my_rows]

    q_up, q_dn, q_sib = [[None, None], [None, None]], [[None, None], [None, None]], [[], []]

    def q_send(part):
        for h in (0, 1):
            q_up[part][h] = send(q_piece(part, y, h), 70 * part + Q_UP + h, to_up)
            q_dn[part][1 - h] = send(q_piece(part, y, 1 - h), 70 * part + Q_DN + 1 - h, to_dn)
        q_sib[part].append(send(q_block(part, y), 70 * part + Q_SIB, to_sib))

    q_fup, q_fdn = [None, None], [None, None]

    def q_forward(part):
        q_up[part][0].wait_recv()
        q_fup[part] = send(q_piece(part, dn, 0), 70 * part + Q_FUP, to_up)
        q_dn[part][1].wait_recv()
        q_fdn[part] = send(q_piece(part, up, 1), 70 * part + Q_FDN, to_dn)

    def q_near(part):
        q_up[part][1].wait_recv()
        q_sib[part].append(send(q_block(part, dn), 70 * part + Q_SIB + 1, to_sib))
        q_dn[part][0].wait_recv()
        q_sib[part].append(send(q_block(part, up), 70 * part + Q_SIB + 2, to_sib))

    def q_far(part):
        q_fup[part].wait_recv()
        q_sib[part].append(send(q_piece(part, opp, 0), 70 * part + Q_SIB + 3, to_sib))
        q_fdn[part].wait_recv()
        q_sib[part].append(send(q_piece(part, opp, 1), 70 * part + Q_SIB + 4, to_sib))

    loads[0].wait()
    loads[1].wait()
    q_send(0)

    loads[3].wait()

    def gather_pages(i, carry):
        for k in range(8):
            leaving[i * 8 + k] = held[send_list[0, (1 - xh) * 8 + i, k]]
            staying[xh, i * 8 + k] = held[send_list[0, xh * 8 + i, k]]
        return carry

    lax.fori_loop(0, 8, gather_pages, 0)

    t_x.wait_recv()
    t_z = []
    for off in range(1, 4):
        t_z.append(send(tok.at[1, my_quarter], T_Z + off - 1, at_z((z + off) % 4)))

    g_x = send(leaving, G_X, to_x, staying.at[xh])

    def o_block(r, chip):
        return wo.at[r, chip, :, my_cols]

    def o_piece(r, chip, h):
        return wo.at[r, chip, pl.ds(h * 512, 512), my_cols]

    q_forward(0)
    loads[2].wait()
    q_send(1)
    loads[4].wait()
    loads[5].wait()
    a_x = send(o_block(1, own_chip), A_X, to_x)
    b_x = [send(o_block(0, own_chip), B_X, to_x)]
    a_sib = [send(o_block(1, own_chip), A_SIB, to_sib)]
    b_sib = [send(o_block(0, own_chip), B_SIB, to_sib)]

    def project(part, which, yy, first=False):
        left = pl.ds(pl.multiple_of(yy * 1024, 1024), 1024)

        def step(n, carry):
            cols = pl.ds(pl.multiple_of(n * 256, 256), 256)
            product = jnp.dot(
                tok[which, :, left], wq[part][yy, :, cols], preferred_element_type=F32)
            acc[part][which, :, cols] = (
                product if first else acc[part][which, :, cols] + product)
            return carry

        lax.fori_loop(0, WIDTH[part] // 256, step, 0)

    loads[6].wait()
    q_sib[0][0].wait_recv()
    project(0, 0, y, True)
    q_near(0)
    q_sib[0][1].wait_recv()
    project(0, 0, dn)
    q_sib[0][2].wait_recv()
    project(0, 0, up)
    q_forward(1)
    q_far(0)

    for copy in t_z:
        copy.wait_recv()
    project(0, 1, y, True)
    project(0, 1, dn)
    project(0, 1, up)
    q_sib[0][3].wait_recv()
    q_sib[0][4].wait_recv()
    project(0, 1, opp)
    psend0[...] = acc0[1].astype(BF16)
    p_x = [send(psend0, P_X, to_x, precv0)]

    q_near(1)
    q_sib[1][0].wait_recv()
    project(1, 1, y, True)
    project(1, 0, y, True)
    q_sib[1][1].wait_recv()
    project(1, 1, dn)
    q_sib[1][2].wait_recv()
    project(1, 1, up)
    q_far(1)

    g_x.wait_recv()
    g_y = []
    my_slot = pl.ds(pl.multiple_of(me * 8, 8), 8)
    for off in range(1, 8):
        there = (me + off) % 8
        slot = pl.ds(pl.multiple_of(there * 8, 8), 8)
        g_y.append(send(
            staying.at[:, slot], G_Y + off - 1, (xh * 8 + there, m), arrived.at[:, my_slot]))
    own_pages = pltpu.make_async_copy(
        staying.at[:, my_slot], arrived.at[:, my_slot], lsem.at[6])
    own_pages.start()
    b_up, b_dn = [None, None], [None, None]
    for h in (0, 1):
        b_up[h] = send(o_piece(0, own_chip, h), B_UP + h, to_up)
        b_dn[1 - h] = send(o_piece(0, own_chip, 1 - h), B_DN + 1 - h, to_dn)

    q_sib[1][3].wait_recv()
    q_sib[1][4].wait_recv()
    project(1, 1, opp)
    psend1[...] = acc1[1].astype(BF16)
    p_x.append(send(psend1, P_X + 66, to_x, precv1))
    project(0, 0, opp)
    project(1, 0, dn)
    project(1, 0, up)
    project(1, 0, opp)

    a_x.wait_recv()
    a_sib.append(send(o_block(1, partner_chip), A_SIB + 1, to_sib))
    b_x[0].wait_recv()
    b_sib.append(send(o_block(0, partner_chip), B_SIB + 1, to_sib))

    diagonal = (
        lax.broadcasted_iota(jnp.int32, (128, 128), 0)
        == lax.broadcasted_iota(jnp.int32, (128, 128), 1))
    lane = lax.broadcasted_iota(jnp.int32, (1, 128), 1)
    inverse = jnp.exp((lane % 64).astype(F32) * (-2.0 / 128.0 * LOG_BASE))
    position = jnp.sum(
        jnp.where(diagonal, row_lengths[...].astype(F32), 0.0), axis=1, keepdims=True)
    tables = []
    for t in range(2):
        angle = (position + float(t)) * inverse
        tables.append((jnp.cos(angle), jnp.where(lane < 64, -1.0, 1.0) * jnp.sin(angle)))

    for copy in g_y:
        copy.wait_recv()
    own_pages.wait()
    append = [
        pltpu.make_async_copy(
            arrived.at[k], held.at[pl.ds(1024 + 64 * k, 64)], lsem.at[7 + k])
        for k in range(2)
    ]
    for copy in append:
        copy.start()

    b_up[0].wait_recv()
    b_fup = send(o_piece(0, xh * 4 + dn, 0), B_FUP, to_up)
    b_dn[1].wait_recv()
    b_fdn = send(o_piece(0, xh * 4 + up, 1), B_FDN, to_dn)
    a_up, a_dn = [[None, None], [None, None]], [[None, None], [None, None]]
    for h in (0, 1):
        for k, chip in enumerate((own_chip, partner_chip)):
            a_up[k][h] = send(o_piece(1, chip, h), A_UP + 2 * k + h, to_up)
            a_dn[k][1 - h] = send(o_piece(1, chip, 1 - h), A_DN + 2 * k + 1 - h, to_dn)

    for copy in p_x:
        copy.wait_recv()
    for t in range(2):
        rows = pl.ds(t * 128, 128)
        cos, sin = tables[t]

        def whole(part, first):
            cols = pl.ds(first, HD)
            return acc[part][0, rows, cols] + precv[part][rows, cols].astype(F32)

        def rotated(value):
            turned = jnp.concatenate([value[:, 64:], value[:, :64]], axis=1)
            return (value * cos + turned * sin).astype(BF16).astype(F32)

        k_new[rows, :] = rotated(whole(0, 0))
        v_new[rows, :] = whole(0, HD).astype(BF16).astype(F32)
        for h in range(4):
            q3[:, t * 8 + h, :] = rotated(whole(0, (h + 2) * HD))
            q3[:, t * 8 + 4 + h, :] = rotated(whole(1, h * HD))
    for copy in append:
        copy.wait()

    b_up[1].wait_recv()
    b_sib.append(send(o_block(0, xh * 4 + dn), B_SIB + 2, to_sib))
    b_x.append(send(o_block(0, xh * 4 + dn), B_X + 1, to_x))
    b_dn[0].wait_recv()
    b_sib.append(send(o_block(0, xh * 4 + up), B_SIB + 3, to_sib))
    b_x.append(send(o_block(0, xh * 4 + up), B_X + 2, to_x))

    scale = 1.0 / HD**0.5
    place = lax.broadcasted_iota(jnp.int32, (16, 128), 1)
    second = lax.broadcasted_iota(jnp.int32, (GROUP * 16, 1), 0) % 16 >= 8

    def attend(i, carry):
        base = i * GROUP
        query = q3[pl.ds(pl.multiple_of(base, GROUP), GROUP)].reshape(GROUP * 16, HD)
        query_low = query.astype(BF16)

        def spread(ref, t):
            value = ref[pl.ds(pl.multiple_of(t * 128 + base, GROUP), GROUP), :]
            return jnp.broadcast_to(
                value[:, None, :], (GROUP, 16, HD)).reshape(GROUP * 16, HD)

        new0 = jnp.sum(query * spread(k_new, 0), axis=1, keepdims=True) * scale
        new1 = jnp.sum(query * spread(k_new, 1), axis=1, keepdims=True) * scale
        new1 = jnp.where(second, new1, -jnp.inf)
        caches = [
            jnp.concatenate([held[table[base + k, j]] for j in range(8)], axis=0)
            for k in range(GROUP)
        ]
        scores = [
            lax.dot_general(
                query_low[k * 16:(k + 1) * 16], caches[k][:, :HD], (((1,), (1,)), ((), ())),
                preferred_element_type=F32)
            for k in range(GROUP)
        ]
        scores = jnp.concatenate([
            jnp.where(place < lengths[base + k], scores[k] * scale, -jnp.inf)
            for k in range(GROUP)], axis=0)
        top = jnp.maximum(jnp.max(scores, axis=1, keepdims=True), jnp.maximum(new0, new1))
        weights = jnp.exp(scores - top)
        weight0 = jnp.exp(new0 - top)
        weight1 = jnp.exp(new1 - top)
        total = jnp.sum(weights, axis=1, keepdims=True) + weight0 + weight1
        weights = weights.astype(BF16)
        numer = jnp.concatenate([
            jnp.dot(weights[k * 16:(k + 1) * 16], caches[k][:, HD:], preferred_element_type=F32)
            for k in range(GROUP)], axis=0)
        numer = numer + weight0.astype(BF16).astype(F32) * spread(v_new, 0)
        numer = numer + weight1.astype(BF16).astype(F32) * spread(v_new, 1)
        q3[pl.ds(pl.multiple_of(base, GROUP), GROUP)] = (numer / total).reshape(GROUP, 16, HD)
        return carry

    lax.fori_loop(0, 128 // GROUP, attend, 0)
    for t in range(2):
        for h in range(8):
            attn[pl.ds(t * 128, 128), pl.ds(h * HD, HD)] = q3[:, t * 8 + h, :].astype(BF16)

    halves = (pl.ds(0, 128), pl.ds(128, 128))

    def z_remote(src, dst, r, chip, h, sem, device):
        return pltpu.make_async_remote_copy(
            src_ref=src, dst_ref=dst, send_sem=z_ssem.at[r, chip, h], recv_sem=sem,
            device_id=device, device_id_type=MESH)

    def far_copy(r, chip, h):
        return z_remote(
            part.at[r, chip, halves[h]], zmid.at[r, h, chip % 2], r, chip, h,
            mid_rsem.at[r, h, chip % 2], at_z(z_up if h else z_dn))

    def near_copy(r, chip, side, h):
        rows = pl.ds(pl.multiple_of(h * 128, 128), 128)
        return z_remote(
            part.at[r, chip, rows], zrecv.at[r, side, chip % 2, rows], r, chip, h,
            z_rsem.at[r, side, chip % 2, h], at_z((z + 3 + 2 * side) % 4))

    def distance(chip):
        return (z - chip // 2 + 4) % 4

    def unit(r, chip):
        for n in range(2):
            cols = pl.ds(n * 256, 256)
            part[r, chip, :, cols] = jnp.dot(
                attn[...], wo[r, chip, :, cols], preferred_element_type=F32).astype(BF16)
        d = distance(chip)

        @pl.when(d == 2)
        def _():
            far_copy(r, chip, 0).start()
            far_copy(r, chip, 1).start()

        @pl.when(d % 2 == 1)
        def _():
            side = d // 2
            near_copy(r, chip, side, 1 - side).start()

    def late(r, chip):
        d = distance(chip)

        @pl.when(d % 2 == 1)
        def _():
            side = d // 2
            rows = pl.ds(pl.multiple_of(side * 128, 128), 128)
            landing = zmid.at[r, side, chip % 2]
            pltpu.make_async_copy(landing, landing, mid_rsem.at[r, side, chip % 2]).wait()
            part[r, chip, rows] = (
                part[r, chip, rows].astype(F32) + zmid[r, side, chip % 2].astype(F32)
            ).astype(BF16)
            near_copy(r, chip, side, side).start()

    waiting = []

    def run(r, chip):
        unit(r, chip)
        waiting.append((r, chip))
        if len(waiting) > 2:
            late(*waiting.pop(0))

    b_fup.wait_recv()
    b_x.append(send(o_piece(0, xh * 4 + opp, 0), B_X + 3, to_x))
    b_sib.append(send(o_piece(0, xh * 4 + opp, 0), B_SIB + 4, to_sib))
    b_fdn.wait_recv()
    b_x.append(send(o_piece(0, xh * 4 + opp, 1), B_X + 4, to_x))
    b_sib.append(send(o_piece(0, xh * 4 + opp, 1), B_SIB + 5, to_sib))
    a_sib[0].wait_recv()
    run(1, own_chip)
    b_sib[0].wait_recv()
    run(0, own_chip)
    a_fup, a_fdn = [], []
    for k, side in enumerate((xh, 1 - xh)):
        a_up[k][0].wait_recv()
        a_fup.append(send(o_piece(1, side * 4 + dn, 0), A_FUP + k, to_up))
        a_dn[k][1].wait_recv()
        a_fdn.append(send(o_piece(1, side * 4 + up, 1), A_FDN + k, to_dn))
    a_sib[1].wait_recv()
    run(1, partner_chip)
    b_sib[1].wait_recv()
    run(0, partner_chip)
    b_sib[2].wait_recv()
    run(0, xh * 4 + dn)
    b_sib[3].wait_recv()
    run(0, xh * 4 + up)
    b_sib[4].wait_recv()
    b_sib[5].wait_recv()
    run(0, xh * 4 + opp)

    for k, side in enumerate((xh, 1 - xh)):
        a_up[k][1].wait_recv()
        a_sib.append(send(o_block(1, side * 4 + dn), A_SIB + 2 + 2 * k, to_sib))
        a_dn[k][0].wait_recv()
        a_sib.append(send(o_block(1, side * 4 + up), A_SIB + 3 + 2 * k, to_sib))
        b_x[1 + k].wait_recv()
        chip = (1 - xh) * 4 + (dn, up)[k]
        b_sib.append(send(o_block(0, chip), B_SIB + 6 + k, to_sib))
        a_sib[2 + 2 * k].wait_recv()
        run(1, side * 4 + dn)
        a_sib[3 + 2 * k].wait_recv()
        run(1, side * 4 + up)
        b_sib[6 + k].wait_recv()
        run(0, chip)
    for h in (0, 1):
        b_x[3 + h].wait_recv()
        b_sib.append(send(o_piece(0, (1 - xh) * 4 + opp, h), B_SIB + 8 + h, to_sib))
    b_sib[8].wait_recv()
    b_sib[9].wait_recv()
    run(0, (1 - xh) * 4 + opp)
    for k, side in enumerate((xh, 1 - xh)):
        a_fup[k].wait_recv()
        a_sib.append(send(o_piece(1, side * 4 + opp, 0), A_SIB + 6 + 2 * k, to_sib))
        a_fdn[k].wait_recv()
        a_sib.append(send(o_piece(1, side * 4 + opp, 1), A_SIB + 7 + 2 * k, to_sib))
        a_sib[6 + 2 * k].wait_recv()
        a_sib[7 + 2 * k].wait_recv()
        run(1, side * 4 + opp)
        if k == 0:
            while waiting and waiting[0][0] == 0:
                late(*waiting.pop(0))
    for pair in waiting:
        late(*pair)

    def z_sum(r, lo):
        total = part[r, z * 2 + lo].astype(F32)
        for side in range(2):
            total = total + zrecv[r, side, lo].astype(F32)
        return total

    def z_wait(r, lo):
        for side in range(2):
            for h in range(2):
                landing = zrecv.at[r, side, lo, halves[h]]
                pltpu.make_async_copy(landing, landing, z_rsem.at[r, side, lo, h]).wait()

    r_x = []
    for r in range(2):
        z_wait(r, 1 - xl)
        xsend[r] = z_sum(r, 1 - xl).astype(BF16)
        r_x.append(send(xsend.at[r], R_X + r, to_lo, xrecv.at[r]))
    for r in range(2):
        z_wait(r, xl)
        r_x[r].wait_recv()
        total = (z_sum(r, xl) + xrecv[r].astype(F32)).astype(BF16)
        for core in range(2):
            out[:, pl.ds(core * 512 + r * 256, 256)] = total[:, core * 256:(core + 1) * 256]

    for copy in sent:
        copy.wait_send()
    for r in range(2):
        for chip in range(8):
            @pl.when(distance(chip) != 0)
            def _():
                for h in range(2):
                    rows = part.at[r, chip, halves[h]]
                    pltpu.make_async_copy(rows, rows, z_ssem.at[r, chip, h]).wait()


def per_device(tokens, q_weight, kv_weight, o_weight, kv_pool, send_list, page_table, lengths):
    rows = tokens.shape[1]
    hbm = pl.BlockSpec(memory_space=pl.ANY)
    vmem = pl.BlockSpec(memory_space=pltpu.VMEM)
    smem = pl.BlockSpec(memory_space=pltpu.SMEM)
    mixed = pl.pallas_call(
        kernel,
        out_shape=jax.ShapeDtypeStruct((256, 1024), BF16),
        in_specs=[hbm] * 5 + [vmem] + [smem] * 3,
        out_specs=vmem,
        scratch_shapes=[
            pltpu.VMEM((4, 1024, WIDTH[0]), BF16),
            pltpu.VMEM((4, 1024, WIDTH[1]), BF16),
            pltpu.VMEM((2, 8, 1024, 512), BF16),
            pltpu.VMEM((2, 256, 4096), BF16),
            pltpu.VMEM((1152, 16, 256), BF16),
            pltpu.VMEM((2, 64, 16, 256), BF16),
            pltpu.VMEM((64, 16, 256), BF16),
            pltpu.VMEM((2, 64, 16, 256), BF16),
            pltpu.VMEM((2, 256, WIDTH[0]), F32),
            pltpu.VMEM((2, 256, WIDTH[1]), F32),
            pltpu.VMEM((256, WIDTH[0]), BF16),
            pltpu.VMEM((256, WIDTH[1]), BF16),
            pltpu.VMEM((256, WIDTH[0]), BF16),
            pltpu.VMEM((256, WIDTH[1]), BF16),
            pltpu.VMEM((128, 16, 128), F32),
            pltpu.VMEM((256, 128), F32),
            pltpu.VMEM((256, 128), F32),
            pltpu.VMEM((256, 1024), BF16),
            pltpu.VMEM((2, 8, 256, 512), BF16),
            pltpu.VMEM((2, 2, 2, 128, 512), BF16),
            pltpu.VMEM((2, 2, 2, 256, 512), BF16),
            pltpu.VMEM((2, 256, 512), BF16),
            pltpu.VMEM((2, 256, 512), BF16),
            pltpu.SemaphoreType.DMA((N_REMOTE,)),
            pltpu.SemaphoreType.DMA((N_REMOTE,)),
            pltpu.SemaphoreType.DMA((2, 8, 2)),
            pltpu.SemaphoreType.DMA((2, 2, 2)),
            pltpu.SemaphoreType.DMA((2, 2, 2, 2)),
            pltpu.SemaphoreType.DMA((10,)),
        ],
        compiler_params=pltpu.CompilerParams(
            collective_id=0, has_side_effects=True, vmem_limit_bytes=62 * 2**20),
    )(
        tokens.reshape(2 * rows, tokens.shape[2]), q_weight, kv_weight, o_weight, kv_pool,
        lengths.reshape(1, rows), send_list, page_table, lengths,
    )
    return mixed.reshape(2, rows, -1)


def solution(mesh):
    in_specs = (
        P(None, "group", None),
        P("group", "mp"),
        P("group", "mp"),
        P("mp", "group"),
        P("group", None, "mp"),
        P("group", None, None),
        P("group", None),
        P("group"),
    )
    out_specs = P(None, "group", "mp")
    return jax.shard_map(
        per_device, mesh=mesh, in_specs=in_specs, out_specs=out_specs, check_vma=False
    )
```

time: 413 us -> 159 us (0.38)
  waiting for transfers between devices: 253 us -> 0 us
  Pallas kernels: 0 us -> 153 us
  local copies, waits for them, and re-layouts: 80.4 us -> 4.63 us
  matrix products: 40.2 us -> 0 us
  other arithmetic: 15.4 us -> 0 us
  between operations: 13.3 us -> 0.01 us
  starting transfers between devices: 7.23 us -> 0 us
    pallas_call x0 -> x1, Pallas kernels: none -> 153 us  [per_device(): pl.pallas_call(kernel, out_shape=jax.ShapeDtypeStruct((256, 1024), BF16),...]
    all_gather x3 -> x0, waiting for transfers between devices: 145 us -> none  [the longest x1 73.8 us: per_device(): query = add_rows(lax.all_gather(q_weight, 'group', axis=0, tiled=True))]
    reduce_scatter x1 -> x0, waiting for transfers between devices: 91.4 us -> none  [per_device(): lax.psum_scatter(partial_term.astype(jnp.bfloat16), 'mp', scatter_dimensi...]
    dot_general x7 -> x0, matrix products: 40.2 us -> none  [the longest x2 14.8 us: add_rows(): return jnp.dot(flat, piece, preferred_element_type=jnp.float32)]
    dot_general x2 -> x0, local copies, waits for them, and re-layouts: 27.9 us -> none  [add_rows(): return jnp.dot(flat, piece, preferred_element_type=jnp.float32)]
    slice x1 -> x0, local copies, waits for them, and re-layouts: 20.1 us -> none  [per_device(): key_cache = cache[:, :, :, 0]]
    gather x2 -> x0, local copies, waits for them, and re-layouts: 18.7 us -> none  [the longest x1 13.7 us: per_device(): cache = held[page_table].reshape(rows, context, kv_here, 2, HD)]
    all_to_all x1 -> x0, waiting for transfers between devices: 14.4 us -> none  [per_device(): lax.all_to_all(outgoing, 'group', split_axis=0, concat_axis=0, tiled=True)]
  transfers between devices with their start and end apart: 5 -> 0, of which waited for: 4 -> 0; matrix products, arithmetic and copies ran while one was open for 30% -> 0% of each run, Pallas kernels for 0% -> 0%
where the time goes in v2:
time: 159 us; the launch traced here: 158 us
  Pallas kernels  153 us (96%)
  local copies, waits for them, and re-layouts  4.63 us (3%)
    pallas_call x1, Pallas kernels, per_device(): pl.pallas_call(kernel, out_shape=jax.ShapeDtypeStruct((256, 1024), BF16),...  153 us
    unnamed x3, local copies, waits for them, and re-layouts  4.63 us

profile of v2, /device:TPU:30, one launch (start us, length us, event | category | flops | bytes accessed | tf_op | source)
XLA Modules:
  0.0 157.7 jit_solution(13714989500359403068)
XLA Ops:
  0.0 1.3 copy.9.send_list
  1.3 1.4 copy.10.table
  2.8 153.0 %shard_map.82 = bf16[256,1024]{1,0:T(8,128)(2,1)} custom-call(bf16[256,8192]{1,0:T(8,128)(2,1)} %bitcast.3, bf16[512,1024]{1,0:T(8,128)(2,1)} %q_weight.1, bf16[512,256]{1,0:T(8,128)(2,1)} %kv_weight.1, bf16[1024,512]{1,0:T(8,128)(2,1)} %o_weight.1, bf16[1024,16,256]{2,1,0:T(8,128)(2,1)} %pool.1, s32[1,128]{1,0:T(1,128)} %bitcast.5, ...), custom_call_target="tpu_custom_call" | custom-call | tf_op jit(solution)/shard_map/pallas_call | solution.py:515
  155.8 1.9 %copy.12 = bf16[2,128,1024]{2,1,0:T(8,128)(2,1)} copy(bf16[2,128,1024]{2,1,0:T(8,128)(2,1)} %bitcast.4) | data formatting | bytes 1048576

commit v3 on v2

--- a/solution.py
+++ b/solution.py
@@ -16,20 +16,25 @@
 T_X, T_Z, P_X, G_X, G_Y = 11, 12, 15, 16, 17
 B_UP, B_DN, B_FUP, B_FDN, B_X, B_SIB = 24, 26, 28, 29, 30, 35
 A_X, A_UP, A_DN, A_FUP, A_FDN, A_SIB = 45, 46, 50, 54, 56, 58
-R_X = 68
-N_REMOTE = 82
+R_X = 82
+N_REMOTE = 116
+FIRST = (0, 256, 384)
+SPAN = (256, 128, 128)
 WIDTH = (768, 512)
 
 
 def kernel(
     tokens, q_weight, kv_weight, o_weight, pool, row_lengths, send_list, table, lengths, out,
-    wq0, wq1, wo, tok, held, arrived, leaving, staying, acc0, acc1, psend0, psend1, precv0, precv1, q3, k_new, v_new, attn,
-    part, zmid, zrecv, xsend, xrecv,
+    wq0, wq1, wo0, wo1, wo2, tok, held, arrived, leaving, staying, acc0, acc1, psend0, psend1, precv0, precv1, q3, k_new, v_new, attn,
+    part0, part1, part2, zmid0, zmid1, zmid2, zrecv0, zrecv1, zrecv2,
+    xsend0, xsend1, xsend2, xrecv0, xrecv1, xrecv2,
     ssem, rsem, z_ssem, mid_rsem, z_rsem, lsem,
 ):
     g = lax.axis_index("group")
     m = lax.axis_index("mp")
     wq, acc, psend, precv = (wq0, wq1), (acc0, acc1), (psend0, psend1), (precv0, precv1)
+    wo, part, zmid = (wo0, wo1, wo2), (part0, part1, part2), (zmid0, zmid1, zmid2)
+    zrecv, xsend, xrecv = (zrecv0, zrecv1, zrecv2), (xsend0, xsend1, xsend2), (xrecv0, xrecv1, xrecv2)
     xh, y, c = g // 8, (g // 2) % 4, g % 2
     z, xl = m // 2, m % 2
     up, dn, opp = (y + 1) % 4, (y + 3) % 4, (y + 2) % 4
@@ -49,7 +54,7 @@
     half = pl.multiple_of(xh * 4096, 4096)
     other_half = pl.multiple_of((1 - xh) * 4096, 4096)
     my_rows = pl.ds(pl.multiple_of(c * 512, 512), 512)
-    my_cols = pl.ds(pl.multiple_of(c * 256, 256), 256)
+    my_cols = [pl.ds(pl.multiple_of(c * span, span), span) for span in SPAN]
     own_chip, partner_chip = xh * 4 + y, (1 - xh) * 4 + y
     loads = [
         pltpu.make_async_copy(kv_weight, wq0.at[y, my_rows, pl.ds(0, 256)], lsem.at[0]),
@@ -57,13 +62,15 @@
             q_weight.at[:, pl.ds(0, 512)], wq0.at[y, my_rows, pl.ds(256, 512)], lsem.at[1]),
         pltpu.make_async_copy(q_weight.at[:, pl.ds(512, 512)], wq1.at[y, my_rows], lsem.at[9]),
         pltpu.make_async_copy(pool, held.at[pl.ds(0, 1024)], lsem.at[2]),
-        pltpu.make_async_copy(
-            o_weight.at[:, pl.ds(256, 256)], wo.at[1, own_chip, :, my_cols], lsem.at[3]),
-        pltpu.make_async_copy(
-            o_weight.at[:, pl.ds(0, 256)], wo.at[0, own_chip, :, my_cols], lsem.at[4]),
         pltpu.make_async_copy(tokens.at[:, pl.ds(half, 4096)], tok.at[0], lsem.at[5]),
     ]
-    for load in loads:
+    o_loads = [
+        pltpu.make_async_copy(
+            o_weight.at[:, pl.ds(FIRST[r], SPAN[r])], wo[r].at[own_chip, :, my_cols[r]],
+            lsem.at[10 + r])
+        for r in range(3)
+    ]
+    for load in loads + o_loads:
         load.start()
 
     barrier = pltpu.get_barrier_semaphore()
@@ -148,19 +155,21 @@
     g_x = send(leaving, G_X, to_x, staying.at[xh])
 
     def o_block(r, chip):
-        return wo.at[r, chip, :, my_cols]
+        return wo[r].at[chip, :, my_cols[r]]
 
     def o_piece(r, chip, h):
-        return wo.at[r, chip, pl.ds(h * 512, 512), my_cols]
+        return wo[r].at[chip, pl.ds(h * 512, 512), my_cols[r]]
 
     q_forward(0)
     loads[2].wait()
     q_send(1)
-    loads[4].wait()
-    loads[5].wait()
-    a_x = send(o_block(1, own_chip), A_X, to_x)
+    for load in o_loads:
+        load.wait()
+    a_x, a_sib = {}, {}
+    for r in (1, 2):
+        a_x[r] = send(o_block(r, own_chip), A_X + 45 * (r - 1), to_x)
+        a_sib[r] = [send(o_block(r, own_chip), A_SIB + 45 * (r - 1), to_sib)]
     b_x = [send(o_block(0, own_chip), B_X, to_x)]
-    a_sib = [send(o_block(1, own_chip), A_SIB, to_sib)]
     b_sib = [send(o_block(0, own_chip), B_SIB, to_sib)]
 
     def project(part, which, yy, first=False):
@@ -176,7 +185,7 @@
 
         lax.fori_loop(0, WIDTH[part] // 256, step, 0)
 
-    loads[6].wait()
+    loads[4].wait()
     q_sib[0][0].wait_recv()
     project(0, 0, y, True)
     q_near(0)
@@ -228,14 +237,15 @@
     q_sib[1][4].wait_recv()
     project(1, 1, opp)
     psend1[...] = acc1[1].astype(BF16)
-    p_x.append(send(psend1, P_X + 66, to_x, precv1))
+    p_x.append(send(psend1, P_X + 70, to_x, precv1))
     project(0, 0, opp)
     project(1, 0, dn)
     project(1, 0, up)
     project(1, 0, opp)
 
-    a_x.wait_recv()
-    a_sib.append(send(o_block(1, partner_chip), A_SIB + 1, to_sib))
+    for r in (1, 2):
+        a_x[r].wait_recv()
+        a_sib[r].append(send(o_block(r, partner_chip), A_SIB + 1 + 45 * (r - 1), to_sib))
     b_x[0].wait_recv()
     b_sib.append(send(o_block(0, partner_chip), B_SIB + 1, to_sib))
 
@@ -266,11 +276,41 @@
     b_fup = send(o_piece(0, xh * 4 + dn, 0), B_FUP, to_up)
     b_dn[1].wait_recv()
     b_fdn = send(o_piece(0, xh * 4 + up, 1), B_FDN, to_dn)
-    a_up, a_dn = [[None, None], [None, None]], [[None, None], [None, None]]
-    for h in (0, 1):
-        for k, chip in enumerate((own_chip, partner_chip)):
-            a_up[k][h] = send(o_piece(1, chip, h), A_UP + 2 * k + h, to_up)
-            a_dn[k][1 - h] = send(o_piece(1, chip, 1 - h), A_DN + 2 * k + 1 - h, to_dn)
+    a_up, a_dn, a_fup, a_fdn = {}, {}, {}, {}
+
+    def a_send(r):
+        for h in (0, 1):
+            for k, chip in enumerate((own_chip, partner_chip)):
+                first = 45 * (r - 1) + 2 * k
+                a_up[r, k, h] = send(o_piece(r, chip, h), A_UP + first + h, to_up)
+                a_dn[r, k, 1 - h] = send(o_piece(r, chip, 1 - h), A_DN + first + 1 - h, to_dn)
+
+    def a_forward(r):
+        for k, side in enumerate((xh, 1 - xh)):
+            a_up[r, k, 0].wait_recv()
+            a_fup[r, k] = send(
+                o_piece(r, side * 4 + dn, 0), A_FUP + 45 * (r - 1) + k, to_up)
+            a_dn[r, k, 1].wait_recv()
+            a_fdn[r, k] = send(
+                o_piece(r, side * 4 + up, 1), A_FDN + 45 * (r - 1) + k, to_dn)
+
+    def a_near(r):
+        for k, side in enumerate((xh, 1 - xh)):
+            first = A_SIB + 45 * (r - 1) + 2 + 2 * k
+            a_up[r, k, 1].wait_recv()
+            a_sib[r].append(send(o_block(r, side * 4 + dn), first, to_sib))
+            a_dn[r, k, 0].wait_recv()
+            a_sib[r].append(send(o_block(r, side * 4 + up), first + 1, to_sib))
+
+    def a_far(r):
+        for k, side in enumerate((xh, 1 - xh)):
+            first = A_SIB + 45 * (r - 1) + 6 + 2 * k
+            a_fup[r, k].wait_recv()
+            a_sib[r].append(send(o_piece(r, side * 4 + opp, 0), first, to_sib))
+            a_fdn[r, k].wait_recv()
+            a_sib[r].append(send(o_piece(r, side * 4 + opp, 1), first + 1, to_sib))
+
+    a_send(1)
 
     for copy in p_x:
         copy.wait_recv()
@@ -359,23 +399,23 @@
 
     def far_copy(r, chip, h):
         return z_remote(
-            part.at[r, chip, halves[h]], zmid.at[r, h, chip % 2], r, chip, h,
+            part[r].at[chip, halves[h]], zmid[r].at[h, chip % 2], r, chip, h,
             mid_rsem.at[r, h, chip % 2], at_z(z_up if h else z_dn))
 
     def near_copy(r, chip, side, h):
         rows = pl.ds(pl.multiple_of(h * 128, 128), 128)
         return z_remote(
-            part.at[r, chip, rows], zrecv.at[r, side, chip % 2, rows], r, chip, h,
+            part[r].at[chip, rows], zrecv[r].at[side, chip % 2, rows], r, chip, h,
             z_rsem.at[r, side, chip % 2, h], at_z((z + 3 + 2 * side) % 4))
 
     def distance(chip):
         return (z - chip // 2 + 4) % 4
 
     def unit(r, chip):
-        for n in range(2):
+        for n in range(SPAN[r] // 128):
             cols = pl.ds(n * 256, 256)
-            part[r, chip, :, cols] = jnp.dot(
-                attn[...], wo[r, chip, :, cols], preferred_element_type=F32).astype(BF16)
+            part[r][chip, :, cols] = jnp.dot(
+                attn[...], wo[r][chip, :, cols], preferred_element_type=F32).astype(BF16)
         d = distance(chip)
 
         @pl.when(d == 2)
@@ -395,10 +435,10 @@
         def _():
             side = d // 2
             rows = pl.ds(pl.multiple_of(side * 128, 128), 128)
-            landing = zmid.at[r, side, chip % 2]
+            landing = zmid[r].at[side, chip % 2]
             pltpu.make_async_copy(landing, landing, mid_rsem.at[r, side, chip % 2]).wait()
-            part[r, chip, rows] = (
-                part[r, chip, rows].astype(F32) + zmid[r, side, chip % 2].astype(F32)
+            part[r][chip, rows] = (
+                part[r][chip, rows].astype(F32) + zmid[r][side, chip % 2].astype(F32)
             ).astype(BF16)
             near_copy(r, chip, side, side).start()
 
@@ -407,7 +447,7 @@
     def run(r, chip):
         unit(r, chip)
         waiting.append((r, chip))
-        if len(waiting) > 2:
+        if len(waiting) > 5:
             late(*waiting.pop(0))
 
     b_fup.wait_recv()
@@ -416,94 +456,109 @@
     b_fdn.wait_recv()
     b_x.append(send(o_piece(0, xh * 4 + opp, 1), B_X + 4, to_x))
     b_sib.append(send(o_piece(0, xh * 4 + opp, 1), B_SIB + 5, to_sib))
-    a_sib[0].wait_recv()
-    run(1, own_chip)
+    for r in (1, 2):
+        a_sib[r][0].wait_recv()
+        run(r, own_chip)
     b_sib[0].wait_recv()
     run(0, own_chip)
-    a_fup, a_fdn = [], []
-    for k, side in enumerate((xh, 1 - xh)):
-        a_up[k][0].wait_recv()
-        a_fup.append(send(o_piece(1, side * 4 + dn, 0), A_FUP + k, to_up))
-        a_dn[k][1].wait_recv()
-        a_fdn.append(send(o_piece(1, side * 4 + up, 1), A_FDN + k, to_dn))
-    a_sib[1].wait_recv()
-    run(1, partner_chip)
+    a_forward(1)
+    a_send(2)
+    for r in (1, 2):
+        a_sib[r][1].wait_recv()
+        run(r, partner_chip)
     b_sib[1].wait_recv()
     run(0, partner_chip)
     b_sib[2].wait_recv()
     run(0, xh * 4 + dn)
     b_sib[3].wait_recv()
     run(0, xh * 4 + up)
+    a_near(1)
     b_sib[4].wait_recv()
     b_sib[5].wait_recv()
     run(0, xh * 4 + opp)
 
-    for k, side in enumerate((xh, 1 - xh)):
-        a_up[k][1].wait_recv()
-        a_sib.append(send(o_block(1, side * 4 + dn), A_SIB + 2 + 2 * k, to_sib))
-        a_dn[k][0].wait_recv()
-        a_sib.append(send(o_block(1, side * 4 + up), A_SIB + 3 + 2 * k, to_sib))
+    def run_near(r):
+        for k, side in enumerate((xh, 1 - xh)):
+            a_sib[r][2 + 2 * k].wait_recv()
+            run(r, side * 4 + dn)
+            a_sib[r][3 + 2 * k].wait_recv()
+            run(r, side * 4 + up)
+
+    def run_far(r):
+        for k, side in enumerate((xh, 1 - xh)):
+            a_sib[r][6 + 2 * k].wait_recv()
+            a_sib[r][7 + 2 * k].wait_recv()
+            run(r, side * 4 + opp)
+
+    def flush(left):
+        while len(waiting) > left:
+            late(*waiting.pop(0))
+
+    def z_sum(r, lo):
+        total = part[r][z * 2 + lo].astype(F32)
+        for side in range(2):
+            total = total + zrecv[r][side, lo].astype(F32)
+        return total
+
+    def z_wait(r, lo):
+        for side in range(2):
+            for h in range(2):
+                landing = zrecv[r].at[side, lo, halves[h]]
+                pltpu.make_async_copy(landing, landing, z_rsem.at[r, side, lo, h]).wait()
+
+    r_x = {}
+
+    def reduce_other(r):
+        z_wait(r, 1 - xl)
+        xsend[r][...] = z_sum(r, 1 - xl).astype(BF16)
+        r_x[r] = send(xsend[r], R_X + r, to_lo, xrecv[r])
+
+    def reduce_own(r):
+        z_wait(r, xl)
+        r_x[r].wait_recv()
+        total = (z_sum(r, xl) + xrecv[r][...].astype(F32)).astype(BF16)
+        for core in range(2):
+            out[:, pl.ds(core * 512 + FIRST[r], SPAN[r])] = (
+                total[:, core * SPAN[r]:(core + 1) * SPAN[r]])
+
+    run_near(1)
+    for k, chip in enumerate(((1 - xh) * 4 + dn, (1 - xh) * 4 + up)):
         b_x[1 + k].wait_recv()
-        chip = (1 - xh) * 4 + (dn, up)[k]
         b_sib.append(send(o_block(0, chip), B_SIB + 6 + k, to_sib))
-        a_sib[2 + 2 * k].wait_recv()
-        run(1, side * 4 + dn)
-        a_sib[3 + 2 * k].wait_recv()
-        run(1, side * 4 + up)
+    a_far(1)
+    a_forward(2)
+    for k, chip in enumerate(((1 - xh) * 4 + dn, (1 - xh) * 4 + up)):
         b_sib[6 + k].wait_recv()
         run(0, chip)
+    run_far(1)
     for h in (0, 1):
         b_x[3 + h].wait_recv()
         b_sib.append(send(o_piece(0, (1 - xh) * 4 + opp, h), B_SIB + 8 + h, to_sib))
+    a_near(2)
     b_sib[8].wait_recv()
     b_sib[9].wait_recv()
     run(0, (1 - xh) * 4 + opp)
-    for k, side in enumerate((xh, 1 - xh)):
-        a_fup[k].wait_recv()
-        a_sib.append(send(o_piece(1, side * 4 + opp, 0), A_SIB + 6 + 2 * k, to_sib))
-        a_fdn[k].wait_recv()
-        a_sib.append(send(o_piece(1, side * 4 + opp, 1), A_SIB + 7 + 2 * k, to_sib))
-        a_sib[6 + 2 * k].wait_recv()
-        a_sib[7 + 2 * k].wait_recv()
-        run(1, side * 4 + opp)
-        if k == 0:
-            while waiting and waiting[0][0] == 0:
-                late(*waiting.pop(0))
-    for pair in waiting:
-        late(*pair)
-
-    def z_sum(r, lo):
-        total = part[r, z * 2 + lo].astype(F32)
-        for side in range(2):
-            total = total + zrecv[r, side, lo].astype(F32)
-        return total
-
-    def z_wait(r, lo):
-        for side in range(2):
-            for h in range(2):
-                landing = zrecv.at[r, side, lo, halves[h]]
-                pltpu.make_async_copy(landing, landing, z_rsem.at[r, side, lo, h]).wait()
-
-    r_x = []
-    for r in range(2):
-        z_wait(r, 1 - xl)
-        xsend[r] = z_sum(r, 1 - xl).astype(BF16)
-        r_x.append(send(xsend.at[r], R_X + r, to_lo, xrecv.at[r]))
-    for r in range(2):
-        z_wait(r, xl)
-        r_x[r].wait_recv()
-        total = (z_sum(r, xl) + xrecv[r].astype(F32)).astype(BF16)
-        for core in range(2):
-            out[:, pl.ds(core * 512 + r * 256, 256)] = total[:, core * 256:(core + 1) * 256]
+    run_near(2)
+    flush(4)
+    a_far(2)
+    run_far(2)
+    flush(2)
+    reduce_other(1)
+    reduce_other(0)
+    flush(0)
+    reduce_other(2)
+    reduce_own(1)
+    reduce_own(0)
+    reduce_own(2)
 
     for copy in sent:
         copy.wait_send()
-    for r in range(2):
+    for r in range(3):
         for chip in range(8):
             @pl.when(distance(chip) != 0)
             def _():
                 for h in range(2):
-                    rows = part.at[r, chip, halves[h]]
+                    rows = part[r].at[chip, halves[h]]
                     pltpu.make_async_copy(rows, rows, z_ssem.at[r, chip, h]).wait()
 
 
@@ -520,7 +575,7 @@
         scratch_shapes=[
             pltpu.VMEM((4, 1024, WIDTH[0]), BF16),
             pltpu.VMEM((4, 1024, WIDTH[1]), BF16),
-            pltpu.VMEM((2, 8, 1024, 512), BF16),
+            *[pltpu.VMEM((8, 1024, 2 * span), BF16) for span in SPAN],
             pltpu.VMEM((2, 256, 4096), BF16),
             pltpu.VMEM((1152, 16, 256), BF16),
             pltpu.VMEM((2, 64, 16, 256), BF16),
@@ -536,17 +591,16 @@
             pltpu.VMEM((256, 128), F32),
             pltpu.VMEM((256, 128), F32),
             pltpu.VMEM((256, 1024), BF16),
-            pltpu.VMEM((2, 8, 256, 512), BF16),
-            pltpu.VMEM((2, 2, 2, 128, 512), BF16),
-            pltpu.VMEM((2, 2, 2, 256, 512), BF16),
-            pltpu.VMEM((2, 256, 512), BF16),
-            pltpu.VMEM((2, 256, 512), BF16),
+            *[pltpu.VMEM((8, 256, 2 * span), BF16) for span in SPAN],
+            *[pltpu.VMEM((2, 2, 128, 2 * span), BF16) for span in SPAN],
+            *[pltpu.VMEM((2, 2, 256, 2 * span), BF16) for span in SPAN],
+            *[pltpu.VMEM((256, 2 * span), BF16) for span in SPAN * 2],
             pltpu.SemaphoreType.DMA((N_REMOTE,)),
             pltpu.SemaphoreType.DMA((N_REMOTE,)),
-            pltpu.SemaphoreType.DMA((2, 8, 2)),
-            pltpu.SemaphoreType.DMA((2, 2, 2)),
-            pltpu.SemaphoreType.DMA((2, 2, 2, 2)),
-            pltpu.SemaphoreType.DMA((10,)),
+            pltpu.SemaphoreType.DMA((3, 8, 2)),
+            pltpu.SemaphoreType.DMA((3, 2, 2)),
+            pltpu.SemaphoreType.DMA((3, 2, 2, 2)),
+            pltpu.SemaphoreType.DMA((13,)),
         ],
         compiler_params=pltpu.CompilerParams(
             collective_id=0, has_side_effects=True, vmem_limit_bytes=62 * 2**20),

time: 159 us -> 150 us (0.943)
  Pallas kernels: 153 us -> 144 us
    pallas_call x1, Pallas kernels: 153 us -> 144 us  [per_device(): pl.pallas_call(kernel, out_shape=jax.ShapeDtypeStruct((256, 1024), BF16),...]
where the time goes in v3:
time: 150 us; the launch traced here: 148 us
  Pallas kernels  144 us (96%)
  local copies, waits for them, and re-layouts  4.63 us (3%)
    pallas_call x1, Pallas kernels, per_device(): pl.pallas_call(kernel, out_shape=jax.ShapeDtypeStruct((256, 1024), BF16),...  144 us
    unnamed x3, local copies, waits for them, and re-layouts  4.63 us

profile of v3, /device:TPU:30, one launch (start us, length us, event | category | flops | bytes accessed | tf_op | source)
XLA Modules:
  0.0 148.3 jit_solution(1065782519546356329)
XLA Ops:
  0.0 1.3 copy.9.send_list
  1.3 1.4 copy.10.table
  2.8 143.6 %shard_map.82 = bf16[256,1024]{1,0:T(8,128)(2,1)} custom-call(bf16[256,8192]{1,0:T(8,128)(2,1)} %bitcast.3, bf16[512,1024]{1,0:T(8,128)(2,1)} %q_weight.1, bf16[512,256]{1,0:T(8,128)(2,1)} %kv_weight.1, bf16[1024,512]{1,0:T(8,128)(2,1)} %o_weight.1, bf16[1024,16,256]{2,1,0:T(8,128)(2,1)} %pool.1, s32[1,128]{1,0:T(1,128)} %bitcast.5, ...), custom_call_target="tpu_custom_call" | custom-call | tf_op jit(solution)/shard_map/pallas_call | solution.py:570
  146.4 1.9 %copy.12 = bf16[2,128,1024]{2,1,0:T(8,128)(2,1)} copy(bf16[2,128,1024]{2,1,0:T(8,128)(2,1)} %bitcast.4) | data formatting | bytes 1048576

commit v4 on v3

--- a/solution.py
+++ b/solution.py
@@ -54,7 +54,6 @@
     half = pl.multiple_of(xh * 4096, 4096)
     other_half = pl.multiple_of((1 - xh) * 4096, 4096)
     my_rows = pl.ds(pl.multiple_of(c * 512, 512), 512)
-    my_cols = [pl.ds(pl.multiple_of(c * span, span), span) for span in SPAN]
     own_chip, partner_chip = xh * 4 + y, (1 - xh) * 4 + y
     loads = [
         pltpu.make_async_copy(kv_weight, wq0.at[y, my_rows, pl.ds(0, 256)], lsem.at[0]),
@@ -66,7 +65,7 @@
     ]
     o_loads = [
         pltpu.make_async_copy(
-            o_weight.at[:, pl.ds(FIRST[r], SPAN[r])], wo[r].at[own_chip, :, my_cols[r]],
+            o_weight.at[:, pl.ds(FIRST[r], SPAN[r])], wo[r].at[own_chip, c],
             lsem.at[10 + r])
         for r in range(3)
     ]
@@ -155,10 +154,10 @@
     g_x = send(leaving, G_X, to_x, staying.at[xh])
 
     def o_block(r, chip):
-        return wo[r].at[chip, :, my_cols[r]]
+        return wo[r].at[chip, c]
 
     def o_piece(r, chip, h):
-        return wo[r].at[chip, pl.ds(h * 512, 512), my_cols[r]]
+        return wo[r].at[chip, c, pl.ds(h * 512, 512)]
 
     q_forward(0)
     loads[2].wait()
@@ -215,8 +214,6 @@
     project(1, 1, dn)
     q_sib[1][2].wait_recv()
     project(1, 1, up)
-    q_far(1)
-
     g_x.wait_recv()
     g_y = []
     my_slot = pl.ds(pl.multiple_of(me * 8, 8), 8)
@@ -232,6 +229,8 @@
     for h in (0, 1):
         b_up[h] = send(o_piece(0, own_chip, h), B_UP + h, to_up)
         b_dn[1 - h] = send(o_piece(0, own_chip, 1 - h), B_DN + 1 - h, to_dn)
+
+    q_far(1)
 
     q_sib[1][3].wait_recv()
     q_sib[1][4].wait_recv()
@@ -414,8 +413,12 @@
     def unit(r, chip):
         for n in range(SPAN[r] // 128):
             cols = pl.ds(n * 256, 256)
+            if SPAN[r] == 256:
+                weight = wo[r][chip, n]
+            else:
+                weight = jnp.concatenate([wo[r][chip, 0], wo[r][chip, 1]], axis=1)
             part[r][chip, :, cols] = jnp.dot(
-                attn[...], wo[r][chip, :, cols], preferred_element_type=F32).astype(BF16)
+                attn[...], weight, preferred_element_type=F32).astype(BF16)
         d = distance(chip)
 
         @pl.when(d == 2)
@@ -541,9 +544,9 @@
     run_near(2)
     flush(4)
     a_far(2)
+    reduce_other(1)
     run_far(2)
     flush(2)
-    reduce_other(1)
     reduce_other(0)
     flush(0)
     reduce_other(2)
@@ -575,7 +578,7 @@
         scratch_shapes=[
             pltpu.VMEM((4, 1024, WIDTH[0]), BF16),
             pltpu.VMEM((4, 1024, WIDTH[1]), BF16),
-            *[pltpu.VMEM((8, 1024, 2 * span), BF16) for span in SPAN],
+            *[pltpu.VMEM((8, 2, 1024, span), BF16) for span in SPAN],
             pltpu.VMEM((2, 256, 4096), BF16),
             pltpu.VMEM((1152, 16, 256), BF16),
             pltpu.VMEM((2, 64, 16, 256), BF16),

time: 150 us -> 150 us (level)
  no operation moved by 1% of the time
where the time goes in v4:
time: 150 us; the launch traced here: 149 us
  Pallas kernels  144 us (96%)
  local copies, waits for them, and re-layouts  4.63 us (3%)
    pallas_call x1, Pallas kernels, per_device(): pl.pallas_call(kernel, out_shape=jax.ShapeDtypeStruct((256, 1024), BF16),...  144 us
    unnamed x3, local copies, waits for them, and re-layouts  4.63 us

profile of v4, /device:TPU:30, one launch (start us, length us, event | category | flops | bytes accessed | tf_op | source)
XLA Modules:
  0.0 148.8 jit_solution(8934854230285141777)
XLA Ops:
  0.0 1.3 copy.9.send_list
  1.3 1.4 copy.10.table
  2.8 144.1 %shard_map.82 = bf16[256,1024]{1,0:T(8,128)(2,1)} custom-call(bf16[256,8192]{1,0:T(8,128)(2,1)} %bitcast.3, bf16[512,1024]{1,0:T(8,128)(2,1)} %q_weight.1, bf16[512,256]{1,0:T(8,128)(2,1)} %kv_weight.1, bf16[1024,512]{1,0:T(8,128)(2,1)} %o_weight.1, bf16[1024,16,256]{2,1,0:T(8,128)(2,1)} %pool.1, s32[1,128]{1,0:T(1,128)} %bitcast.5, ...), custom_call_target="tpu_custom_call" | custom-call | tf_op jit(solution)/shard_map/pallas_call | solution.py:573
  146.9 1.9 %copy.12 = bf16[2,128,1024]{2,1,0:T(8,128)(2,1)} copy(bf16[2,128,1024]{2,1,0:T(8,128)(2,1)} %bitcast.4) | data formatting | bytes 1048576
